TPU v7x, 32 devices: a whole 2x2x4 slice. The times are simulated.
32 devices in a mesh: batch: 1, blk: 4 (over x, core), box: 8 (over z, y).
Axes of the slice: x: 2, y: 2, z: 4, core: 2. Of those that a mesh axis runs over, the one named last changes fastest.
Arguments:
- surface_points: float32 [3, 4096], P(None, ('blk', 'box')), may hold values from -4 to 4
- angle_ids: int32 [128], P('batch'), may hold values from 0 to 16383
- near_mask: int32 [32, 8], P(('blk', 'box')), may hold values 0 or 1
- skeleton: int32 [32, 32], P(('blk', 'box')), may hold values from 0 to 127, as said below
- box_inverse_parts: float32 [32, 2, 128, 128], P(('blk', 'box')), may hold values from -0.375 to 0.375
- near_coupling: float32 [32, 8, 2, 32, 128], P(('blk', 'box')), may hold values from -0.25 to 0.25
- top_inverse: float32 [4, 2, 256, 256], P('blk', None, 'box'), may hold values from -0.25 to 0.25
Outputs:
- scattered: float32 [2, 128, 4096], P(None, ('batch', 'box'), 'blk')
Inputs may be any that keep to these rules, and one draw needn't show every extreme that they name: `skeleton`: each row holds 32 distinct row numbers of a box.
All inputs are finite; a program needn't handle non-finite values. No bound on the sum of `near_mask` on one device may be relied on, other than what follows from the above.
Results may differ from a plain program's by a relative error of at most 0.0003.
Values sent between devices are 32-bit elements; how exact they have to be, the bound alone decides.
No kernel may reach another device: no remote copies, remote signals or barrier semaphores. Data moves between devices by JAX's collectives and lax.ppermute only.
A program may use at most 64 MiB of HBM per device.

v0:
```python
import jax
import jax.numpy as jnp
from jax import lax
from jax.sharding import PartitionSpec as P

SWEEP = 16384


wavenumber = 24.0
offsets = ((-1, -1), (-1, 0), (-1, 1), (0, -1), (0, 1), (1, -1), (1, 0), (1, 1))


def extended(cells, sides, width):
    for axis, dim in sides:
        count = lax.axis_size(axis)
        head = lax.slice_in_dim(cells, 0, width, axis=dim)
        tail = lax.slice_in_dim(cells, cells.shape[dim] - width, cells.shape[dim], axis=dim)
        cells = jnp.concatenate(
            [
                lax.ppermute(tail, axis, [(i, (i + 1) % count) for i in range(count)]),
                cells,
                lax.ppermute(head, axis, [((i + 1) % count, i) for i in range(count)]),
            ],
            axis=dim,
        )
    return cells


def incident(points, angles):
    theta = angles.astype(jnp.float32) * (2.0 * jnp.pi / SWEEP)
    phase = wavenumber * (
        points[0][:, None] * jnp.cos(theta)[None, :]
        + points[1][:, None] * (0.6 * jnp.sin(theta))[None, :]
        + points[2][:, None] * (0.8 * jnp.sin(theta))[None, :]
    )
    return jnp.stack([jnp.cos(phase), jnp.sin(phase)])


def complex_multiply(form, mat_re, mat_im, vec_re, vec_im):
    first = jnp.einsum(form, mat_re, vec_re, precision=lax.Precision.HIGHEST) - jnp.einsum(
        form, mat_im, vec_im, precision=lax.Precision.HIGHEST
    )
    second = jnp.einsum(form, mat_re, vec_im, precision=lax.Precision.HIGHEST) + jnp.einsum(
        form, mat_im, vec_re, precision=lax.Precision.HIGHEST
    )
    return (first, second)


def on_device(
    surface_points, angle_ids, near_mask, skeleton, box_inverse_parts, near_coupling, top_inverse
):
    boxes = box_inverse_parts.shape[0]
    width = box_inverse_parts.shape[2]
    count = angle_ids.shape[0]
    rank = skeleton.shape[1]
    field = incident(surface_points, angle_ids)
    field = field.reshape(2, boxes, width, count)
    one_hot_picker = (skeleton[:, :, None] == jnp.arange(width)[None, None, :]).astype(jnp.float32)
    zre, zim = complex_multiply(
        "jrc,jca->jra", box_inverse_parts[:, 0], box_inverse_parts[:, 1], field[0], field[1]
    )
    skel_values = jnp.einsum(
        "ipb,cibq->icpq", one_hot_picker, jnp.stack([zre, zim]), precision=lax.Precision.HIGHEST
    )
    padded = extended(skel_values[None], (("blk", 0), ("box", 1)), 1)
    nearby = jnp.stack(
        [padded[1 + step_s, 1 + step_q : 1 + step_q + boxes] for step_s, step_q in offsets]
    )
    weights = near_coupling * near_mask.astype(jnp.float32)[:, :, None, None, None]
    cre, cim = complex_multiply(
        "jmkr,mjka->jra", weights[:, :, 0], weights[:, :, 1], nearby[:, :, 0], nearby[:, :, 1]
    )
    weight_real = zre - cre
    wim = zim - cim
    tops = jnp.einsum(
        "ipb,cibq->cipq",
        one_hot_picker,
        jnp.stack([weight_real, wim]),
        precision=lax.Precision.HIGHEST,
    ).reshape(2, boxes * rank, count)
    matrix = top_inverse[0]
    piece = lax.all_gather(tops, "box", axis=1, tiled=True)
    part_re, part_im = complex_multiply("rc,ca->ra", matrix[0], matrix[1], piece[0], piece[1])
    solved_values = jnp.stack([part_re, part_im])
    solved_values = solved_values.reshape(2, boxes, rank, count)
    vector_real = weight_real + jnp.einsum(
        "ipb,ipq->ibq", one_hot_picker, solved_values[0], precision=lax.Precision.HIGHEST
    )
    vector_imaginary = wim + jnp.einsum(
        "ipb,ipq->ibq", one_hot_picker, solved_values[1], precision=lax.Precision.HIGHEST
    )
    solution_real, solution_imaginary = complex_multiply(
        "wxf,wxo->owf",
        box_inverse_parts[:, 0],
        box_inverse_parts[:, 1],
        vector_real,
        vector_imaginary,
    )
    result = jnp.stack(
        [
            solution_real.reshape(count, boxes * width),
            solution_imaginary.reshape(count, boxes * width),
        ]
    )
    return lax.all_to_all(result, "box", split_axis=1, concat_axis=2, tiled=True)


def solution(mesh):
    return jax.shard_map(
        on_device,
        mesh=mesh,
        in_specs=(
            P(None, ("blk", "box")),
            P("batch"),
            P(("blk", "box"), None),
            P(("blk", "box"), None),
            P(("blk", "box"), None, None, None),
            P(("blk", "box"), None, None, None, None),
            P("blk", None, "box", None),
        ),
        out_specs=P(None, ("batch", "box"), "blk"),
        check_vma=False,
    )
```

profile of v0, /device:TPU:0, one launch (start us, length us, event | category | flops | bytes accessed | tf_op | source)
XLA Modules:
  0.0 65.8 jit_solution(15142796924028334679)
XLA Ops:
  0.0 0.7 %fusion.86 = (f32[128]{0:T(128)S(1)}, f32[128]{0:T(128)S(1)}, f32[128]{0:T(128)S(1)}) fusion(s32[128]{0:T(128)} %param.8), kind=kLoop, calls=%fused_computation.121 | loop fusion | flops 512 | bytes 2048 | tf_op jit(solution)/shard_map/cos | solution.py:32
  0.8 1.4 %fusion.24 = f32[128,128]{1,0:T(8,128)S(1)} fusion(f32[1,2,128,128]{3,2,1,0:T(8,128)} %param.11, f32[128]{0:T(128)S(1)} %get-tuple-element.9, f32[128]{0:T(128)S(1)} %get-tuple-element.6, f32[128]{0:T(128)S(1)} %get-tuple-element.10, f32[128]{0:T(128)S(1)} %get-tuple-element.7, f32[128]{0:T(128)S(1)} %get-tuple-element.8, f32[128]{0:T(128)S(1)} %get-tuple-element.5), kind=kOutput, calls=%fused_computation.49 | convolution fusion | flops 25264128 | bytes 134144 | tf_op jit(solution)/shard_map/jrc,jca->jra/dot_general | solution.py:40
  2.2 0.6 fusion.16
  2.8 0.6 convolution_subtract_fusion.1
  3.3 0.6 convolution_add_fusion.3
  3.9 0.2 convolution_bitcast_fusion.5
  4.2 0.5 collective-permute-start
  4.7 2.0 %collective-permute-start.1 = (f32[1,1,2,32,128]{4,3,2,1,0:T(8,128)S(1)}, f32[1,1,2,32,128]{4,3,2,1,0:T(8,128)S(1)}, u32[]{:S(2)}, u32[]{:S(2)}) collective-permute-start(f32[1,1,2,32,128]{4,3,2,1,0:T(8,128)S(1)} %convolution_bitcast_fusion.5), channel_id=1, source_target_pairs={{8,0},{16,8},{24,16},{0,24},{9,1},{17,9},{25,17},{1,25},{10,2},{18... | collective-permute-start | bytes 98312 | tf_op jit(solution)/shard_map/ppermute | solution.py:22
  6.7 1.5 %collective-permute-done = f32[1,1,2,32,128]{4,3,2,1,0:T(8,128)S(1)} collective-permute-done((f32[1,1,2,32,128]{4,3,2,1,0:T(8,128)S(1)}, f32[1,1,2,32,128]{4,3,2,1,0:T(8,128)S(1)}, u32[]{:S(2)}, u32[]{:S(2)}) %collective-permute-start) | collective-permute-done | bytes 32800 | tf_op jit(solution)/shard_map/ppermute | solution.py:20
  8.4 2.2 %collective-permute-start.2 = (f32[3,1,2,32,128]{4,3,2,1,0:T(8,128)S(1)}, f32[3,1,2,32,128]{4,3,2,1,0:T(8,128)S(1)}, u32[]{:S(2)}, u32[]{:S(2)}) collective-permute-start(f32[3,1,2,32,128]{4,3,2,1,0:T(8,128)S(1)} %pad_maximum_fusion.1), channel_id=1, source_target_pairs={{0,1},{1,2},{2,3},{3,4},{4,5},{5,6},{6,7},{7,0},{8,9},{9,10},{10,1... | collective-permute-start | bytes 294920 | tf_op jit(solution)/shard_map/ppermute | solution.py:20
  10.7 3.1 %collective-permute-start.3 = (f32[3,1,2,32,128]{4,3,2,1,0:T(8,128)S(1)}, f32[3,1,2,32,128]{4,3,2,1,0:T(8,128)S(1)}, u32[]{:S(2)}, u32[]{:S(2)}) collective-permute-start(f32[3,1,2,32,128]{4,3,2,1,0:T(8,128)S(1)} %pad_maximum_fusion.1), channel_id=1, source_target_pairs={{1,0},{2,1},{3,2},{4,3},{5,4},{6,5},{7,6},{0,7},{9,8},{10,9},{11,1... | collective-permute-start | bytes 294920 | tf_op jit(solution)/shard_map/ppermute | solution.py:22
  13.8 2.7 %collective-permute-done.2 = f32[3,1,2,32,128]{4,3,2,1,0:T(8,128)S(1)} collective-permute-done((f32[3,1,2,32,128]{4,3,2,1,0:T(8,128)S(1)}, f32[3,1,2,32,128]{4,3,2,1,0:T(8,128)S(1)}, u32[]{:S(2)}, u32[]{:S(2)}) %collective-permute-start.2) | collective-permute-done | bytes 98336 | tf_op jit(solution)/shard_map/ppermute | solution.py:20
  16.5 1.8 %collective-permute-done.3 = f32[3,1,2,32,128]{4,3,2,1,0:T(8,128)S(1)} collective-permute-done((f32[3,1,2,32,128]{4,3,2,1,0:T(8,128)S(1)}, f32[3,1,2,32,128]{4,3,2,1,0:T(8,128)S(1)}, u32[]{:S(2)}, u32[]{:S(2)}) %collective-permute-start.3) | collective-permute-done | bytes 98336 | tf_op jit(solution)/shard_map/ppermute | solution.py:22
  18.3 0.4 convolution_bitcast_fusion.3
  18.7 0.4 convolution_bitcast_fusion.1
  19.1 0.4 fusion.4
  19.5 0.4 fusion.5
  19.9 0.2 convolution_bitcast_fusion.4
  20.1 31.1 %all-gather = f32[2,1,256,128]{3,2,0,1:T(8,128)S(1)} all-gather(f32[2,1,32,128]{3,2,0,1:T(8,128)S(1)} %convolution_bitcast_fusion.4), channel_id=2, replica_groups=mesh['batch'=1,'blk'=4,'box'=8] {'box'}, dimensions={2}, use_global_device_ids=true | all-gather | bytes 294912 | tf_op jit(solution)/shard_map/all_gather | solution.py:82
  51.8 0.3 convolution_add_fusion.2
  52.5 0.3 convolution_add_fusion.1
  53.0 0.2 fusion.1
  53.5 11.5 %all_to_all.18 = f32[2,128,128]{2,0,1:T(2,128)S(1)} all-to-all(f32[2,128,128]{2,0,1:T(2,128)S(1)} %copy.38), channel_id=1, replica_groups=mesh['batch'=1,'blk'=4,'box'=8] {'box'}, dimensions={1} | all-to-all | bytes 262144 | tf_op jit(solution)/shard_map/all_to_all | solution.py:105
  65.2 0.7 %all_to_all.16 = f32[2,16,1024]{2,1,0:T(8,128)} reshape(f32[2,16,8,128]{3,2,1,0:T(8,128)S(1)} %copy.39) | data formatting | bytes 262144 | tf_op jit(solution)/shard_map/all_to_all | solution.py:105
  (35 shorter events, 1.9 us)
Async XLA Ops:
  0.0 0.7 %copy-start.4 = (f32[3,128]{1,0:T(4,128)S(1)}, f32[3,128]{1,0:T(4,128)}, u32[]{:S(2)}) copy-start(f32[3,128]{1,0:T(4,128)} %param.7) | copy-start | bytes 4612
  0.0 2.2 %copy-start = (f32[1,2,128,128]{3,2,1,0:T(8,128)S(1)}, f32[1,2,128,128]{3,2,1,0:T(8,128)}, u32[]{:S(2)}) copy-start(f32[1,2,128,128]{3,2,1,0:T(8,128)} %param.11) | copy-start | bytes 393220
  2.7 1.2 %copy-start.3 = (s32[1,32]{1,0:T(1,128)S(1)}, s32[1,32]{1,0:T(1,128)}, u32[]{:S(2)}) copy-start(s32[1,32]{1,0:T(1,128)} %param.10) | copy-start | bytes 388
  3.3 7.3 %copy-start.1 = (f32[1,8,2,32,128]{4,3,2,1,0:T(8,128)S(1)}, f32[1,8,2,32,128]{4,3,2,1,0:T(8,128)}, u32[]{:S(2)}) copy-start(f32[1,8,2,32,128]{4,3,2,1,0:T(8,128)} %param.12) | copy-start | bytes 786436
  3.9 2.7 %copy-start.5 = (s32[1,8]{1,0:T(1,128)S(1)}, s32[1,8]{1,0:T(1,128)}, u32[]{:S(2)}) copy-start(s32[1,8]{1,0:T(1,128)} %param.9) | copy-start | bytes 100
  4.2 4.0 %collective-permute-start = (f32[1,1,2,32,128]{4,3,2,1,0:T(8,128)S(1)}, f32[1,1,2,32,128]{4,3,2,1,0:T(8,128)S(1)}, u32[]{:S(2)}, u32[]{:S(2)}) collective-permute-start(f32[1,1,2,32,128]{4,3,2,1,0:T(8,128)S(1)} %convolution_bitcast_fusion.5), channel_id=1, source_target_pairs={{0,8},{8,16},{16,24},{24,0},{1,9},{9,17},{17,25},{25,1},{2,10},{10... | collective-permute-start | bytes 98312 | tf_op jit(solution)/shard_map/ppermute | solution.py:20
  4.7 3.7 %collective-permute-start.1 = (f32[1,1,2,32,128]{4,3,2,1,0:T(8,128)S(1)}, f32[1,1,2,32,128]{4,3,2,1,0:T(8,128)S(1)}, u32[]{:S(2)}, u32[]{:S(2)}) collective-permute-start(f32[1,1,2,32,128]{4,3,2,1,0:T(8,128)S(1)} %convolution_bitcast_fusion.5), channel_id=1, source_target_pairs={{8,0},{16,8},{24,16},{0,24},{9,1},{17,9},{25,17},{1,25},{10,2},{18... | collective-permute-start | bytes 98312 | tf_op jit(solution)/shard_map/ppermute | solution.py:22
  8.4 8.1 %collective-permute-start.2 = (f32[3,1,2,32,128]{4,3,2,1,0:T(8,128)S(1)}, f32[3,1,2,32,128]{4,3,2,1,0:T(8,128)S(1)}, u32[]{:S(2)}, u32[]{:S(2)}) collective-permute-start(f32[3,1,2,32,128]{4,3,2,1,0:T(8,128)S(1)} %pad_maximum_fusion.1), channel_id=1, source_target_pairs={{0,1},{1,2},{2,3},{3,4},{4,5},{5,6},{6,7},{7,0},{8,9},{9,10},{10,1... | collective-permute-start | bytes 294920 | tf_op jit(solution)/shard_map/ppermute | solution.py:20
  10.7 7.6 %collective-permute-start.3 = (f32[3,1,2,32,128]{4,3,2,1,0:T(8,128)S(1)}, f32[3,1,2,32,128]{4,3,2,1,0:T(8,128)S(1)}, u32[]{:S(2)}, u32[]{:S(2)}) collective-permute-start(f32[3,1,2,32,128]{4,3,2,1,0:T(8,128)S(1)} %pad_maximum_fusion.1), channel_id=1, source_target_pairs={{1,0},{2,1},{3,2},{4,3},{5,4},{6,5},{7,6},{0,7},{9,8},{10,9},{11,1... | collective-permute-start | bytes 294920 | tf_op jit(solution)/shard_map/ppermute | solution.py:22
  20.1 31.1 %copy-start.2 = (f32[1,2,32,256]{3,2,1,0:T(8,128)S(1)}, f32[1,2,32,256]{3,2,1,0:T(8,128)}, u32[]{:S(2)}) copy-start(f32[1,2,32,256]{3,2,1,0:T(8,128)} %param.13) | copy-start | bytes 196612
where the time goes:
time: 66.1 us; the launch traced here: 65.8 us
  blocking collectives  42.6 us (64%)
  starting transfers between devices  7.83 us (12%)
  matrix products  7.19 us (11%)
  waiting for transfers between devices  6.14 us (9%)
  local copies, waits for them, and re-layouts  0.94 us (1%)
  other arithmetic  0.84 us (1%)
    all_gather x1, blocking collectives, on_device(): piece = lax.all_gather(tops, 'box', axis=1, tiled=True)  31.1 us
    all_to_all x1, blocking collectives, on_device(): lax.all_to_all(result, 'box', split_axis=1, concat_axis=2, tiled=True)  11.5 us
    ppermute x2, starting transfers between devices, extended(): lax.ppermute(head, axis, [((i + 1) % count, i) for i in range(count)])  5.11 us
    ppermute x2, waiting for transfers between devices, extended(): lax.ppermute(tail, axis, [(i, (i + 1) % count) for i in range(count)])  4.21 us
    ppermute x2, starting transfers between devices, extended(): lax.ppermute(tail, axis, [(i, (i + 1) % count) for i in range(count)])  2.72 us
    dot_general x4, matrix products, complex_multiply(): jnp.einsum(form, mat_re, vec_re, precision=lax.Precision.HIGHEST)  2.18 us
    ppermute x2, waiting for transfers between devices, extended(): lax.ppermute(head, axis, [((i + 1) % count, i) for i in range(count)])  1.92 us
    dot_general x4, matrix products, complex_multiply(): jnp.einsum(form, mat_im, vec_im, precision=lax.Precision.HIGHEST)  1.34 us
  transfers between devices with their start and end apart: 4, of which 4 were waited for; matrix products, arithmetic and copies ran while one was open for 0% of the time, Pallas kernels for 0%

commit v1 on v0

v1 whole, which is shorter than its diff:
```python
import functools

import jax
import jax.numpy as jnp
import numpy as np
from jax import lax
from jax.experimental import pallas as pl
from jax.experimental.pallas import tpu as pltpu
from jax.sharding import PartitionSpec as P

SWEEP = 16384
WAVENUMBER = 24.0
F32 = jnp.float32
BF16 = jnp.bfloat16
VMEM = pl.BlockSpec(memory_space=pltpu.VMEM)
NN = (((1,), (0,)), ((), ()))
NT = (((1,), (1,)), ((), ()))
TN = (((0,), (0,)), ((), ()))

HALF_PI_1 = float(np.float32(201.0 / 128.0))
HALF_PI_2 = float(np.float32(np.round((np.pi / 2 - HALF_PI_1) * 2.0**22) / 2.0**22))
HALF_PI_3 = float(np.float32(np.pi / 2 - HALF_PI_1 - HALF_PI_2))


def cat(parts, axis):
    return jnp.concatenate(parts, axis=axis)


def dot(a, b, form=NN):
    return lax.dot_general(a, b, form, preferred_element_type=F32)


def split(x):
    high = x.astype(BF16)
    return high, (x - high.astype(F32)).astype(BF16)


def dot3(a, b, form=NN):
    return dot(a[0], b[0], form) + (dot(a[0], b[1], form) + dot(a[1], b[0], form))


def both(pair, function):
    return function(pair[0]), function(pair[1])


def sin_cos_small(r):
    s = r * r
    sin = r + r * s * (-1.6666654611e-1 + s * (8.3321608736e-3 - s * 1.9515295891e-4))
    cos = 1.0 - 0.5 * s + s * s * (4.166664568298827e-2 + s * (-1.388731625493765e-3 + s * 2.443315711809948e-5))
    return sin, cos


def by_quadrant(quadrant, sin, cos):
    odd = (quadrant & 1) == 1
    out_sin = jnp.where(odd, cos, sin)
    out_cos = jnp.where(odd, sin, cos)
    out_sin = jnp.where((quadrant & 2) == 2, -out_sin, out_sin)
    out_cos = jnp.where(((quadrant + 1) & 2) == 2, -out_cos, out_cos)
    return out_sin, out_cos


def one_hot(skeleton, width):
    rows = lax.broadcasted_iota(jnp.int32, (width, skeleton.shape[1]), 0)
    return jnp.where(rows == skeleton, 1.0, 0.0).astype(BF16)


def rows_form(re, im):
    return cat([cat([re, -im], 1), cat([im, re], 1)], 0)


def columns_form(re, im):
    return cat([cat([re, im], 1), cat([-im, re], 1)], 0)


def field_kernel(points, angles, skeleton, inverse, top, u_out, static_out, high_out, low_out):
    count = angles.shape[1]
    width = points.shape[1]
    rank = skeleton.shape[1]
    ids = angles[...]
    quadrant = (ids + SWEEP // 8) >> (SWEEP.bit_length() - 3)
    rest = ids - quadrant * (SWEEP // 4)
    sin, cos = by_quadrant(quadrant, *sin_cos_small(rest.astype(F32) * (2.0 * np.pi / SWEEP)))
    pick = lax.broadcasted_iota(jnp.int32, (8, count), 0) == 0
    columns = jnp.where(pick, cos, sin).T
    cos_column = columns[:, 0:1]
    sin_column = columns[:, 1:2]
    x = points[0:1, :] * WAVENUMBER
    yz = points[1:2, :] * (0.6 * WAVENUMBER) + points[2:3, :] * (0.8 * WAVENUMBER)
    phase = x * cos_column + yz * sin_column
    turns = jnp.round(phase * (2.0 / np.pi))
    r = ((phase - turns * HALF_PI_1) - turns * HALF_PI_2) - turns * HALF_PI_3
    field_sin, field_cos = by_quadrant(turns.astype(jnp.int32), *sin_cos_small(r))
    field = split(cat([field_cos, field_sin], 1))
    high_out[...] = field[0]
    low_out[...] = field[1]
    parts = split(cat([inverse[0, 0], inverse[0, 1]], 1))
    picker = one_hot(skeleton[...], width)
    rows = dot(picker, cat(parts, 1), TN)
    rows_high = rows[:, : 2 * width]
    rows_low = rows[:, 2 * width :]
    whole = rows_high + rows_low
    form = both((rows_high, rows_low), lambda v: rows_form(v[:, :width], v[:, width:]).astype(BF16))
    u_out[...] = dot3(form, field, NT)
    depth = top.shape[3]
    for part in range(2):
        at = slice(part * rank, (part + 1) * rank)
        static_out[at, :depth] = top[0, part]
        static_out[at, depth:] = whole[:, part * width : (part + 1) * width]


def coupling_kernel(high, low, skeleton, mask, inverse, coupling, base_out, high_out, low_out):
    width = inverse.shape[2]
    sides = coupling.shape[1]
    rank = coupling.shape[3]
    depth = sides * rank
    field = (high[...], low[...])
    re = split(inverse[0, 0])
    im = split(inverse[0, 1])
    row_matrix = (rows_form(re[0], im[0]), rows_form(re[1], im[1]))
    column_matrix = (columns_form(re[0], im[0]), columns_form(re[1], im[1]))
    picker = one_hot(skeleton[...], width)
    zero = jnp.zeros_like(picker)
    picker2 = cat([cat([picker, zero], 1), cat([zero, picker], 1)], 0)
    z = split(dot3(field, row_matrix, NT))
    u = dot(z[0], picker2) + dot(z[1], picker2)
    near = []
    for side in range(sides):
        weight = mask[0, side].astype(F32)
        near.append(cat([coupling[0, side, 0] * weight, coupling[0, side, 1] * weight], 1))
    near = split(cat(near, 0))
    base_out[:, : 2 * width] = dot3(z, column_matrix)
    base_out[:, 2 * width :] = u
    applied = split(dot3(near, column_matrix))
    for k, out in enumerate((high_out, low_out)):
        chosen = dot(near[k], picker2).astype(BF16)
        for matrix, at, part in ((applied[k], 0, width), (chosen, 2 * width, rank)):
            out[:depth, at : at + 2 * part] = matrix
            out[depth:, at : at + part] = -matrix[:, part:]
            out[depth:, at + part : at + 2 * part] = matrix[:, :part]


def message_kernel(up, down, left, right, base, high, low, out):
    boxes = out.shape[0]
    count = base.shape[0]
    width = out.shape[2]
    rank = up.shape[0] // 2
    share = count // boxes
    half = share // 2
    order = (left[0], up[...], right[0], left[1], right[1], left[2], down[...], right[2])
    stacked = cat([v[:rank] for v in order] + [v[rank:] for v in order], 0)
    near = split(stacked.T)
    w = base[...] - dot3(near, (high[...], low[...]))
    for box in range(boxes):
        at = box * share
        out[box, :share] = w[at : at + share, :width]
        out[box, share : 2 * share] = w[at : at + share, width : 2 * width]
        t = w[at : at + share, 2 * width :]
        out[box, 2 * share : 2 * share + half] = cat([t[:half], t[half:]], 1)


def top_kernel(message, static, out):
    boxes = message.shape[0]
    width = message.shape[2]
    share = out.shape[1]
    half = share // 2
    rank = static.shape[1] // 2
    depth = boxes * rank
    t_re = []
    t_im = []
    for box in range(boxes):
        packed = message[box, 2 * share : 2 * share + half]
        t = cat([packed[:, : 2 * rank], packed[:, 2 * rank :]], 0)
        t_re.append(t[:, :rank])
        t_im.append(t[:, rank:])
    t = split(cat(t_re + t_im, 1))
    top = []
    for box in range(boxes):
        top.append(rows_form(static[box, :rank, :depth], static[box, rank:, :depth]))
    y = dot3(t, split(cat(top, 0)), NT)
    for box in range(boxes):
        local = split(columns_form(static[box, :rank, depth:], static[box, rank:, depth:]))
        part = split(y[:, box * 2 * rank : (box + 1) * 2 * rank])
        x = dot3(part, local)
        at = slice(box * width, (box + 1) * width)
        out[0, :, at] = message[box, :share] + x[:, :width]
        out[1, :, at] = message[box, share : 2 * share] + x[:, width:]


def call(kernel, outs, *arrays, smem=()):
    specs = [pl.BlockSpec(memory_space=pltpu.SMEM) if i in smem else VMEM for i in range(len(arrays))]
    return pl.pallas_call(
        kernel,
        out_shape=[jax.ShapeDtypeStruct(shape, dtype) for shape, dtype in outs],
        in_specs=specs,
        out_specs=[VMEM] * len(outs),
        compiler_params=pltpu.CompilerParams(vmem_limit_bytes=40 * 1024 * 1024),
    )(*arrays)


def shifted(value, axis, step):
    count = lax.axis_size(axis)
    return lax.ppermute(value, axis, [(i, (i + step) % count) for i in range(count)])


def on_device(surface_points, angle_ids, near_mask, skeleton, box_inverse_parts, near_coupling, top_inverse):
    boxes = lax.axis_size("box")
    width = box_inverse_parts.shape[2]
    count = angle_ids.shape[0]
    rank = skeleton.shape[1]
    sides = near_mask.shape[1]
    depth = top_inverse.shape[3]
    share = count // boxes
    u, static, high, low = call(
        field_kernel,
        [
            ((2 * rank, count), F32),
            ((2 * rank, depth + width), F32),
            ((count, 2 * width), BF16),
            ((count, 2 * width), BF16),
        ],
        surface_points, angle_ids.reshape(1, count), skeleton, box_inverse_parts, top_inverse,
    )
    up = shifted(u, "blk", 1)
    down = shifted(u, "blk", -1)
    column = jnp.stack([up, u, down])
    left = shifted(column, "box", 1)
    right = shifted(column, "box", -1)
    static = lax.all_gather(static, "box")
    base, matrix_high, matrix_low = call(
        coupling_kernel,
        [
            ((count, 2 * width + 2 * rank), F32),
            ((2 * sides * rank, 2 * width + 2 * rank), BF16),
            ((2 * sides * rank, 2 * width + 2 * rank), BF16),
        ],
        high, low, skeleton, near_mask, box_inverse_parts, near_coupling, smem=(3,),
    )
    rows = 2 * share + -(-share // 16) * 8
    (message,) = call(
        message_kernel, [((boxes, rows, width), F32)],
        up, down, left, right, base, matrix_high, matrix_low,
    )
    message = lax.all_to_all(message, "box", split_axis=0, concat_axis=0, tiled=True)
    (out,) = call(top_kernel, [((2, share, boxes * width), F32)], message, static)
    return out


def solution(mesh):
    return jax.shard_map(
        on_device,
        mesh=mesh,
        in_specs=(
            P(None, ("blk", "box")),
            P("batch"),
            P(("blk", "box"), None),
            P(("blk", "box"), None),
            P(("blk", "box"), None, None, None),
            P(("blk", "box"), None, None, None, None),
            P("blk", None, "box", None),
        ),
        out_specs=P(None, ("batch", "box"), "blk"),
        check_vma=False,
    )
```

time: 66.1 us -> 59.2 us (0.90)
  blocking collectives: 42.6 us -> 34.1 us
  matrix products: 7.19 us -> 0 us
  starting transfers between devices: 7.83 us -> 12.5 us
  Pallas kernels: 0 us -> 4.51 us
  local copies, waits for them, and re-layouts: 0.94 us -> 3.75 us
  waiting for transfers between devices: 6.14 us -> 4.08 us
  other arithmetic: 0.84 us -> 0.01 us
    all_to_all x1 -> x0, blocking collectives: 11.5 us -> none  [on_device(): lax.all_to_all(result, 'box', split_axis=1, concat_axis=2, tiled=True)]
    dot_general x20 -> x0, matrix products: 7.19 us -> none  [the longest x4 2.18 us: complex_multiply(): jnp.einsum(form, mat_re, vec_re, precision=lax.Precision.HIGHEST)]
    all_to_all x0 -> x1, starting transfers between devices: none -> 4.66 us  [on_device(): lax.all_to_all(message, 'box', split_axis=0, concat_axis=0, tiled=True)]
    pallas_call x0 -> x4, Pallas kernels: none -> 4.51 us  [call(): pl.pallas_call(kernel, out_shape=[jax.ShapeDtypeStruct(shape, dtype) for...]
    unnamed x19 -> x16, local copies, waits for them, and re-layouts: 0.06 us -> 3.75 us
    all_gather x1, blocking collectives: 31.1 us -> 34.1 us  [on_device(): static = lax.all_gather(static, 'box')]
    ppermute x4, waiting for transfers between devices: 6.14 us -> 4.08 us  [shifted(): lax.ppermute(value, axis, [(i, (i + step) % count) for i in range(count)])]
    all_to_all x2 -> x0, local copies, waits for them, and re-layouts: 0.76 us -> none  [on_device(): lax.all_to_all(result, 'box', split_axis=1, concat_axis=2, tiled=True)]
  transfers between devices with their start and end apart: 4 -> 5, of which waited for: 4 -> 4; matrix products, arithmetic and copies ran while one was open for 0% -> 0% of each run, Pallas kernels for 0% -> 2%
where the time goes in v1:
time: 59.2 us; the launch traced here: 58.9 us
  blocking collectives  34.1 us (58%)
  starting transfers between devices  12.5 us (21%)
  Pallas kernels  4.51 us (8%)
  waiting for transfers between devices  4.08 us (7%)
  local copies, waits for them, and re-layouts  3.75 us (6%)
    all_gather x1, blocking collectives, on_device(): static = lax.all_gather(static, 'box')  34.1 us
    ppermute x4, starting transfers between devices, shifted(): lax.ppermute(value, axis, [(i, (i + step) % count) for i in range(count)])  7.82 us
    all_to_all x1, starting transfers between devices, on_device(): lax.all_to_all(message, 'box', split_axis=0, concat_axis=0, tiled=True)  4.66 us
    pallas_call x4, Pallas kernels, call(): pl.pallas_call(kernel, out_shape=[jax.ShapeDtypeStruct(shape, dtype) for...  4.51 us
    ppermute x4, waiting for transfers between devices, shifted(): lax.ppermute(value, axis, [(i, (i + step) % count) for i in range(count)])  4.08 us
    unnamed x16, local copies, waits for them, and re-layouts  3.75 us
  transfers between devices with their start and end apart: 5, of which 4 were waited for; matrix products, arithmetic and copies ran while one was open for 0% of the time, Pallas kernels for 2%

profile of v1, /device:TPU:0, one launch (start us, length us, event | category | flops | bytes accessed | tf_op | source)
XLA Modules:
  0.0 58.9 jit_solution(9090278792470409017)
XLA Ops:
  0.0 0.7 %copy-done.6 = s32[128]{0:T(128)S(1)} copy-done((s32[128]{0:T(128)S(1)}, s32[128]{0:T(128)}, u32[]{:S(2)}) %copy-start.6) | copy-done | bytes 536
  0.7 0.0 copy-done.5
  0.7 0.9 %copy-done = f32[1,2,128,128]{3,2,1,0:T(8,128)S(1)} copy-done((f32[1,2,128,128]{3,2,1,0:T(8,128)S(1)}, f32[1,2,128,128]{3,2,1,0:T(8,128)}, u32[]{:S(2)}) %copy-start) | copy-done | bytes 131096
  1.6 0.8 %copy-done.3 = f32[1,2,32,256]{3,2,1,0:T(8,128)S(1)} copy-done((f32[1,2,32,256]{3,2,1,0:T(8,128)S(1)}, f32[1,2,32,256]{3,2,1,0:T(8,128)}, u32[]{:S(2)}) %copy-start.3) | copy-done | bytes 65560
  2.4 0.7 %copy-done.4 = f32[3,128]{1,0:T(4,128)S(1)} copy-done((f32[3,128]{1,0:T(4,128)S(1)}, f32[3,128]{1,0:T(4,128)}, u32[]{:S(2)}) %copy-start.4) | copy-done | bytes 1560
  3.1 0.4 shard_map.73
  3.6 0.0 copy-start.1
  3.6 0.5 collective-permute-start
  4.1 2.0 %collective-permute-start.1 = (f32[64,128]{1,0:T(8,128)S(1)}, f32[64,128]{1,0:T(8,128)S(1)}, u32[]{:S(2)}, u32[]{:S(2)}) collective-permute-start(f32[64,128]{1,0:T(8,128)S(1)} %get-tuple-element.12), channel_id=1, source_target_pairs={{0,24},{8,0},{16,8},{24,16},{1,25},{9,1},{17,9},{25,17},{2,26},{10... | collective-permute-start | bytes 98312 | tf_op jit(solution)/shard_map/ppermute | solution.py:202
  6.1 1.5 %collective-permute-done.up = f32[64,128]{1,0:T(8,128)S(1)} collective-permute-done((f32[64,128]{1,0:T(8,128)S(1)}, f32[64,128]{1,0:T(8,128)S(1)}, u32[]{:S(2)}, u32[]{:S(2)}) %collective-permute-start) | collective-permute-done | bytes 32800 | tf_op jit(solution)/shard_map/ppermute | solution.py:202
  7.6 0.2 collective-permute-done.1.down
  7.8 2.2 %collective-permute-start.2 = (f32[3,64,128]{2,1,0:T(8,128)S(1)}, f32[3,64,128]{2,1,0:T(8,128)S(1)}, u32[]{:S(2)}, u32[]{:S(2)}) collective-permute-start(f32[3,64,128]{2,1,0:T(8,128)S(1)} %pad_maximum_fusion), channel_id=1, source_target_pairs={{0,1},{1,2},{2,3},{3,4},{4,5},{5,6},{6,7},{7,0},{8,9},{9,10},{10,1... | collective-permute-start | bytes 294920 | tf_op jit(solution)/shard_map/ppermute | solution.py:202
  10.0 3.1 %collective-permute-start.3 = (f32[3,64,128]{2,1,0:T(8,128)S(1)}, f32[3,64,128]{2,1,0:T(8,128)S(1)}, u32[]{:S(2)}, u32[]{:S(2)}) collective-permute-start(f32[3,64,128]{2,1,0:T(8,128)S(1)} %pad_maximum_fusion), channel_id=1, source_target_pairs={{0,7},{1,0},{2,1},{3,2},{4,3},{5,4},{6,5},{7,6},{8,15},{9,8},{10,9... | collective-permute-start | bytes 294920 | tf_op jit(solution)/shard_map/ppermute | solution.py:202
  13.1 0.0 copy-done.2
  13.1 0.0 copy-done.1
  13.1 0.6 %copy-done.7 = s32[1,8]{1,0:T(1,128)S(1)} copy-done((s32[1,8]{1,0:T(1,128)S(1)}, s32[1,8]{1,0:T(1,128)}, u32[]{:S(2)}) %copy-start.7) | copy-done | bytes 56
  13.8 1.4 %shard_map.74 = (f32[128,320]{1,0:T(8,128)S(1)}, bf16[512,320]{1,0:T(8,128)(2,1)S(1)}, bf16[512,320]{1,0:T(8,128)(2,1)S(1)}) custom-call(bf16[128,256]{1,0:T(8,128)(2,1)S(1)} %get-tuple-element.13.high, bf16[128,256]{1,0:T(8,128)(2,1)S(1)} %get-tuple-element.14.low, s32[1,32]{1,0:T(1,128)S(1)} %copy-done.5, s32[1,8]{1,0:T(1,128)S(1)} %copy-done.7, ...), custom_call_target="tpu_custom_call" | custom-call | tf_op jit(solution)/shard_map/pallas_call | solution.py:191
  15.1 0.8 %collective-permute-done.2.left = f32[3,64,128]{2,1,0:T(8,128)S(1)} collective-permute-done((f32[3,64,128]{2,1,0:T(8,128)S(1)}, f32[3,64,128]{2,1,0:T(8,128)S(1)}, u32[]{:S(2)}, u32[]{:S(2)}) %collective-permute-start.2) | collective-permute-done | bytes 98336 | tf_op jit(solution)/shard_map/ppermute | solution.py:202
  15.9 1.6 %collective-permute-done.3.right = f32[3,64,128]{2,1,0:T(8,128)S(1)} collective-permute-done((f32[3,64,128]{2,1,0:T(8,128)S(1)}, f32[3,64,128]{2,1,0:T(8,128)S(1)}, u32[]{:S(2)}, u32[]{:S(2)}) %collective-permute-start.3) | collective-permute-done | bytes 98336 | tf_op jit(solution)/shard_map/ppermute | solution.py:202
  17.5 1.2 %shard_map.75 = f32[8,40,128]{2,1,0:T(8,128)} custom-call(f32[64,128]{1,0:T(8,128)S(1)} %collective-permute-done.up, f32[64,128]{1,0:T(8,128)S(1)} %collective-permute-done.1.down, f32[3,64,128]{2,1,0:T(8,128)S(1)} %collective-permute-done.2.left, f32[3,64,128]{2,1,0:T(8,128)S(1)} %collective-permute-done.3.right, f32[128,320]{1,0:T(8,128)S(1)} %get-tuple-element.15.base, ...), custom_call_target="tpu_custom_call" | custom-call | tf_op jit(solution)/shard_map/pallas_call | solution.py:191
  18.7 4.7 %all-to-all-start = ((f32[8,40,128]{2,1,0:T(8,128)}), f32[8,40,128]{2,1,0:T(8,128)S(1)}, u32[]{:S(2)}, u32[]{:S(2)}) async-start(f32[8,40,128]{2,1,0:T(8,128)} %shard_map.75), calls=%async_computation | async-start | bytes 327680 | tf_op jit(solution)/shard_map/all_to_all | solution.py:243
  23.3 34.1 %all-gather = f32[512,384]{1,0:T(8,128)S(1)} all-gather(f32[64,384]{1,0:T(8,128)S(1)} %get-tuple-element.18), channel_id=2, replica_groups=mesh['batch'=1,'blk'=4,'box'=8] {'box'}, dimensions={0}, use_global_device_ids=true | all-gather | bytes 884736 | tf_op jit(solution)/shard_map/all_gather | solution.py:228
  57.4 0.0 all-to-all-done.message
  57.4 1.5 %shard_map.76 = f32[2,16,1024]{2,1,0:T(8,128)} custom-call(f32[8,40,128]{2,1,0:T(8,128)S(1)} %all-to-all-done.message, f32[8,64,384]{2,1,0:T(8,128)S(1)} %bitcast.5), custom_call_target="tpu_custom_call" | custom-call | tf_op jit(solution)/shard_map/pallas_call | solution.py:191
  (8 shorter events, 0.0 us)
Async XLA Ops:
  0.0 0.7 %copy-start.6 = (s32[128]{0:T(128)S(1)}, s32[128]{0:T(128)}, u32[]{:S(2)}) copy-start(s32[128]{0:T(128)} %param.8) | copy-start | bytes 1540
  0.0 0.7 %copy-start.5 = (s32[1,32]{1,0:T(1,128)S(1)}, s32[1,32]{1,0:T(1,128)}, u32[]{:S(2)}) copy-start(s32[1,32]{1,0:T(1,128)} %skeleton.3) | copy-start | bytes 388
  0.7 0.9 %copy-start = (f32[1,2,128,128]{3,2,1,0:T(8,128)S(1)}, f32[1,2,128,128]{3,2,1,0:T(8,128)}, u32[]{:S(2)}) copy-start(f32[1,2,128,128]{3,2,1,0:T(8,128)} %inverse.3) | copy-start | bytes 393220
  1.6 0.8 %copy-start.3 = (f32[1,2,32,256]{3,2,1,0:T(8,128)S(1)}, f32[1,2,32,256]{3,2,1,0:T(8,128)}, u32[]{:S(2)}) copy-start(f32[1,2,32,256]{3,2,1,0:T(8,128)} %top.1) | copy-start | bytes 196612
  2.4 0.7 %copy-start.4 = (f32[3,128]{1,0:T(4,128)S(1)}, f32[3,128]{1,0:T(4,128)}, u32[]{:S(2)}) copy-start(f32[3,128]{1,0:T(4,128)} %points.1) | copy-start | bytes 4612
  3.1 10.0 %copy-start.2 = (f32[1,8,2,32,128]{4,3,2,1,0:T(8,128)S(1)}, f32[1,8,2,32,128]{4,3,2,1,0:T(8,128)}, u32[]{:S(2)}) copy-start(f32[1,8,2,32,128]{4,3,2,1,0:T(8,128)} %coupling.1) | copy-start | bytes 786436
  3.6 9.6 %copy-start.1 = (f32[1,2,128,128]{3,2,1,0:T(8,128)S(1)}, f32[1,2,128,128]{3,2,1,0:T(8,128)}, u32[]{:S(2)}) copy-start(f32[1,2,128,128]{3,2,1,0:T(8,128)} %inverse.3) | copy-start | bytes 393220
  3.6 4.0 %collective-permute-start = (f32[64,128]{1,0:T(8,128)S(1)}, f32[64,128]{1,0:T(8,128)S(1)}, u32[]{:S(2)}, u32[]{:S(2)}) collective-permute-start(f32[64,128]{1,0:T(8,128)S(1)} %get-tuple-element.12), channel_id=1, source_target_pairs={{0,8},{8,16},{16,24},{24,0},{1,9},{9,17},{17,25},{25,1},{2,10},{10... | collective-permute-start | bytes 98312 | tf_op jit(solution)/shard_map/ppermute | solution.py:202
  4.1 3.7 %collective-permute-start.1 = (f32[64,128]{1,0:T(8,128)S(1)}, f32[64,128]{1,0:T(8,128)S(1)}, u32[]{:S(2)}, u32[]{:S(2)}) collective-permute-start(f32[64,128]{1,0:T(8,128)S(1)} %get-tuple-element.12), channel_id=1, source_target_pairs={{0,24},{8,0},{16,8},{24,16},{1,25},{9,1},{17,9},{25,17},{2,26},{10... | collective-permute-start | bytes 98312 | tf_op jit(solution)/shard_map/ppermute | solution.py:202
  7.8 8.1 %collective-permute-start.2 = (f32[3,64,128]{2,1,0:T(8,128)S(1)}, f32[3,64,128]{2,1,0:T(8,128)S(1)}, u32[]{:S(2)}, u32[]{:S(2)}) collective-permute-start(f32[3,64,128]{2,1,0:T(8,128)S(1)} %pad_maximum_fusion), channel_id=1, source_target_pairs={{0,1},{1,2},{2,3},{3,4},{4,5},{5,6},{6,7},{7,0},{8,9},{9,10},{10,1... | collective-permute-start | bytes 294920 | tf_op jit(solution)/shard_map/ppermute | solution.py:202
  10.0 7.5 %collective-permute-start.3 = (f32[3,64,128]{2,1,0:T(8,128)S(1)}, f32[3,64,128]{2,1,0:T(8,128)S(1)}, u32[]{:S(2)}, u32[]{:S(2)}) collective-permute-start(f32[3,64,128]{2,1,0:T(8,128)S(1)} %pad_maximum_fusion), channel_id=1, source_target_pairs={{0,7},{1,0},{2,1},{3,2},{4,3},{5,4},{6,5},{7,6},{8,15},{9,8},{10,9... | collective-permute-start | bytes 294920 | tf_op jit(solution)/shard_map/ppermute | solution.py:202
  13.1 0.7 %copy-start.7 = (s32[1,8]{1,0:T(1,128)S(1)}, s32[1,8]{1,0:T(1,128)}, u32[]{:S(2)}) copy-start(s32[1,8]{1,0:T(1,128)} %mask.1) | copy-start | bytes 100
  18.7 38.7 %all-to-all-start = ((f32[8,40,128]{2,1,0:T(8,128)}), f32[8,40,128]{2,1,0:T(8,128)S(1)}, u32[]{:S(2)}, u32[]{:S(2)}) async-start(f32[8,40,128]{2,1,0:T(8,128)} %shard_map.75), calls=%async_computation | async-start | bytes 327680 | tf_op jit(solution)/shard_map/all_to_all | solution.py:243
